TPU v7x, 32 devices: a whole 2x2x4 slice. The times are simulated.
32 devices in a mesh: seq: 16 (over z, x, core), fsdp: 2 (over y).
Axes of the slice: x: 2, y: 2, z: 4, core: 2. Of those that a mesh axis runs over, the one named last changes fastest.
Arguments:
- state_in: bfloat16 [2048, 5280], P('seq'), may hold values from -6 to 6
- query_vectors: bfloat16 [2048, 2688], P('seq', 'fsdp'), may hold values from -6 to 6
- key_vectors: bfloat16 [2048, 2688], P('seq', 'fsdp'), may hold values from -6 to 6
- value_weight: bfloat16 [2, 1344, 5280], P('fsdp', 'seq'), may hold values from -0.078125 to 0.078125
- out_weight: bfloat16 [2, 1344, 5280], P('fsdp', 'seq'), may hold values from -0.3125 to 0.3125
- doc_ids: int32 [16], replicated, may hold values from 0 to 4, never falling along the last dimension, each value on 1 to 5 neighbouring positions
- cotangent: bfloat16 [2048, 5280], P('seq'), may hold values from -6 to 6
Outputs:
- final_state: bfloat16 [2048, 5280], P('seq')
- state_grad: float32 [2048, 5280], P('seq')
Inputs may be any that keep to these rules, and one draw needn't show every extreme that they name: `doc_ids`: document ids never fall along the blocks; each document covers 1 to 5 consecutive blocks, and some document covers exactly 5.
All inputs are finite; a program needn't handle non-finite values.
Results may differ from a plain program's by a relative error of at most 0.013.
Values may be sent and summed in bfloat16 or wider, within the bound.
A program may use at most 256 MiB of HBM per device.

v0:
```python
import math

import jax
import jax.numpy as jnp
from jax import lax
from jax.sharding import PartitionSpec as P

HEAD_DIM = 96
BLOCK = 128
UNROLL = 2
REACH = 4


epsilon = 1e-06


def from_behind(value, axis, steps):
    count = lax.axis_size(axis)
    first, last = (max(0, -steps), min(count, count - steps))
    return lax.ppermute(value, axis, [(source, source + steps) for source in range(first, last)])


def normalize(current):
    mean_square = jnp.mean(current * current, axis=-1, keepdims=True)
    inverse_rms = lax.rsqrt(mean_square + epsilon)
    return (current * inverse_rms, inverse_rms)


def head_total(partial_value):
    return lax.psum(partial_value.astype(jnp.bfloat16), "fsdp").astype(jnp.float32)


def contract_last(left, right):
    return lax.dot_general(
        left, right, (((1,), (1,)), ((), ())), preferred_element_type=jnp.float32
    )


def fetch_first(pair):
    return [from_behind((pair[0], pair[1]), "seq", distance) for distance in range(REACH, 0, -1)]


def fetch_later(values_b):
    return [from_behind(values_b, "seq", distance) for distance in range(REACH, 0, -1)]


def local(state_in, query_vectors, key_vectors, value_weight, out_weight, doc_ids, cotangent):
    rows_here = state_in.shape[0]
    blocks_here = rows_here // BLOCK
    width_here = query_vectors.shape[1]
    heads_here = width_here // HEAD_DIM
    window_rows = (REACH + 1) * rows_here
    pad_rows = REACH * rows_here
    device_index = lax.axis_index("seq")
    score_scale = 1.0 / math.sqrt(HEAD_DIM)
    doc_padded = jnp.concatenate([jnp.full((REACH * blocks_here,), -1, jnp.int32), doc_ids])
    window_docs = lax.dynamic_slice_in_dim(
        doc_padded, device_index * blocks_here, (REACH + 1) * blocks_here, 0
    )
    key_docs = jnp.broadcast_to(window_docs[:, None], ((REACH + 1) * blocks_here, BLOCK)).reshape(
        -1
    )
    query_docs = key_docs[pad_rows:]
    slot_rows = jnp.arange(window_rows)
    query_rows = jnp.arange(rows_here) + pad_rows
    allowed = (key_docs[None, :] == query_docs[:, None]) & (
        slot_rows[None, :] <= query_rows[:, None]
    )
    gathered_value, gathered_out = (
        lax.all_gather(value_weight, "seq", axis=1, tiled=True),
        lax.all_gather(out_weight, "seq", axis=1, tiled=True),
    )
    value_rows = gathered_value[0]
    out_rows = gathered_out[0]
    current = state_in.astype(jnp.float32)
    records = []
    soft_weights = None
    for unroll_step in range(UNROLL):
        normed, inverse_rms = normalize(current)
        values_b = contract_last(normed.astype(jnp.bfloat16), value_rows).astype(jnp.bfloat16)
        if unroll_step == 0:
            received = fetch_first((key_vectors, values_b))
            window_keys = jnp.concatenate([pair[0] for pair in received] + [key_vectors], 0)
            window_values = jnp.concatenate([pair[1] for pair in received] + [values_b], 0)
            query_heads = query_vectors.reshape(rows_here, heads_here, HEAD_DIM)
            key_heads = window_keys.reshape(window_rows, heads_here, HEAD_DIM)
            scores = (
                jnp.einsum(
                    "qhd,khd->hqk", query_heads, key_heads, preferred_element_type=jnp.float32
                )
                * score_scale
            )
            masked = jnp.where(allowed[None], scores, -1e30)
            maxima = jnp.max(masked, axis=2, keepdims=True)
            raised = jnp.where(allowed[None], jnp.exp(masked - maxima), 0.0)
            denominator = jnp.sum(raised, axis=2, keepdims=True)
            soft_weights = (raised / denominator).astype(jnp.bfloat16)
        else:
            received = fetch_later(values_b)
            window_values = jnp.concatenate(received + [values_b], 0)
        attended = jnp.einsum(
            "hqk,khd->qhd",
            soft_weights,
            window_values.reshape(window_rows, heads_here, HEAD_DIM),
            preferred_element_type=jnp.float32,
        )
        attended = attended.reshape(rows_here, width_here).astype(jnp.bfloat16)
        current = current + head_total(
            jnp.dot(attended, out_rows, preferred_element_type=jnp.float32)
        )
        records.append((normed, inverse_rms))
    final_state = current.astype(jnp.bfloat16)
    gradient = cotangent.astype(jnp.float32)
    for normed, inverse_rms in reversed(records):
        grad_b = gradient.astype(jnp.bfloat16)
        d_attended = contract_last(grad_b, out_rows).astype(jnp.bfloat16)
        slot_terms = jnp.einsum(
            "hqk,qhd->khd",
            soft_weights,
            d_attended.reshape(rows_here, heads_here, HEAD_DIM),
            preferred_element_type=jnp.float32,
        )
        slot_terms = slot_terms.reshape(REACH + 1, rows_here, width_here).astype(jnp.bfloat16)
        returned = [
            from_behind(slot_terms[REACH - distance], "seq", -distance)
            for distance in range(1, REACH + 1)
        ]
        running = slot_terms[REACH].astype(jnp.float32)
        for piece_back in returned:
            running = running + piece_back.astype(jnp.float32)
        dvalues = running.astype(jnp.bfloat16)
        d_normed = head_total(jnp.dot(dvalues, value_rows, preferred_element_type=jnp.float32))
        gradient = gradient + inverse_rms * (
            d_normed - normed * jnp.mean(d_normed * normed, axis=-1, keepdims=True)
        )
    return (final_state, gradient)


def solution(mesh):
    placed = (
        P("seq", None),
        P("seq", "fsdp"),
        P("seq", "fsdp"),
        P("fsdp", "seq", None),
        P("fsdp", "seq", None),
        P(),
        P("seq", None),
    )
    return jax.shard_map(
        local,
        mesh=mesh,
        in_specs=placed,
        out_specs=(P("seq", None), P("seq", None)),
        check_vma=False,
    )
```

profile of v0, /device:TPU:0, one launch (start us, length us, event | category | flops | bytes accessed | tf_op | source)
XLA Modules:
  0.0 660.5 jit_solution(9032868497417658662)
XLA Ops:
  7.2 3.9 copy.19
  11.2 2.6 copy.21
  14.0 5.7 collective-permute-start.4
  19.6 2.6 collective-permute-start.5
  22.2 2.7 collective-permute-start.6
  25.0 2.6 collective-permute-start.7
  30.0 4.3 collective-permute-done.4
  35.4 1.7 collective-permute-done.5
  37.1 14.7 %collective-permute-done.6 = bf16[128,1344]{0,1:T(8,128)(2,1)S(1)} collective-permute-done((bf16[128,1344]{0,1:T(8,128)(2,1)S(1)}, bf16[128,1344]{0,1:T(8,128)(2,1)S(1)}, u32[]{:S(2)}, u32[]{:S(2)}) %collective-permute-start.6) | collective-permute-done | bytes 344096 | tf_op jit(solution)/shard_map/ppermute | solution.py:20
  52.1 1.2 copy-done.16
  53.3 5.6 fusion.82
  58.9 2.9 divide_convert_fusion
  61.8 109.0 %all-gather.3.cloned.1.call-done = bf16[1,1344,5280]{2,0,1:T(2,128)(2,1)} async-done(((bf16[1,84,5280]{2,0,1:T(2,128)(2,1)}), bf16[1,1344,5280]{2,0,1:T(2,128)(2,1)}) %all-gather.3.cloned.1.call-update) | async-done | bytes 14192656 | tf_op jit(solution)/shard_map/all_gather | solution.py:70
  170.8 13.9 %copy.29 = bf16[1,1344,5280]{2,1,0:T(8,128)(2,1)S(1)} copy(bf16[1,1344,5280]{2,0,1:T(2,128)(2,1)} %all-gather.3.cloned.1.call-done) | data formatting | bytes 28385280
  184.7 4.0 fusion.43
  188.6 1.2 copy-done.2
  189.8 2.3 collective-permute-start
  192.1 18.9 %collective-permute-start.1 = (bf16[128,1344]{0,1:T(8,128)(2,1)S(1)}, bf16[128,1344]{0,1:T(8,128)(2,1)}, u32[]{:S(2)}, u32[]{:S(2)}) collective-permute-start(bf16[128,1344]{0,1:T(8,128)(2,1)S(1)} %fusion.43), channel_id=1, source_target_pairs={{0,6},{2,8},{4,10},{6,12},{8,14},{10,16},{12,18},{14,20},{16,22},{... | collective-permute-start | bytes 1032200 | tf_op jit(solution)/shard_map/ppermute | solution.py:20
  210.9 1.7 collective-permute-start.2
  212.7 2.5 collective-permute-start.3
  215.2 127.6 %all-gather.5.cloned.1.call-done = bf16[1,1344,5280]{2,0,1:T(2,128)(2,1)} async-done(((bf16[1,84,5280]{2,0,1:T(2,128)(2,1)}), bf16[1,1344,5280]{2,0,1:T(2,128)(2,1)}) %all-gather.5.cloned.1.call-update) | async-done | bytes 14192656 | tf_op jit(solution)/shard_map/all_gather | solution.py:71
  342.8 13.9 %copy.30 = bf16[1,1344,5280]{2,1,0:T(8,128)(2,1)S(1)} copy(bf16[1,1344,5280]{2,0,1:T(2,128)(2,1)} %all-gather.5.cloned.1.call-done) | data formatting | bytes 28385280
  356.8 4.0 fusion.49
  363.1 1.3 collective-permute-start.15
  364.5 1.3 collective-permute-start.14
  366.8 1.3 collective-permute-start.13
  369.2 1.3 collective-permute-start.12
  371.5 10.8 %fusion.23 = bf16[128,5280]{0,1:T(8,128)(2,1)} fusion(bf16[128,1344]{0,1:T(8,128)(2,1)S(1)} %bitcast.99, bf16[1,1344,5280]{2,1,0:T(8,128)(2,1)} %copy-done.3), kind=kOutput, calls=%fused_computation.19 | convolution fusion | flops 1817333760 | bytes 15888384 | tf_op jit(solution)/shard_map/dot_general | solution.py:109
  382.3 1.7 collective-permute-done.14
  383.9 6.5 collective-permute-done.13
  390.5 10.8 %fusion.17 = bf16[128,5280]{0,1:T(8,128)(2,1)} fusion(bf16[1,1344,5280]{2,1,0:T(8,128)(2,1)} %copy-done.2, bf16[128,1344]{0,1:T(8,128)(2,1)S(1)} %bitcast.97, bf16[128,1344]{0,1:T(8,128)(2,1)S(1)} %collective-permute-done.15, bf16[128,1344]{0,1:T(8,128)(2,1)S(1)} %collective-permute-done.14, bf16[128,1344]{0,1:T(8,128)(2,1)S(1)} %collective-permute-done.13, ...), kind=kOutput, calls=%fused_computation.17 | convolution fusion | flops 1819054080 | bytes 17264640 | tf_op jit(solution)/shard_map/dot_general | solution.py:132
  401.4 88.2 %all-reduce.8.cloned.1.call-done = (bf16[128,5280]{0,1:T(8,128)(2,1)}, bf16[128,5280]{0,1:T(8,128)(2,1)}) async-done(((bf16[128,5280]{0,1:T(8,128)(2,1)}, bf16[128,5280]{0,1:T(8,128)(2,1)}), (bf16[128,5280]{0,1:T(8,128)(2,1)}, bf16[128,5280]{0,1:T(8,128)(2,1)})) %all-reduce.8.cloned.1.call-update) | async-done | bytes 2703376 | tf_op jit(solution)/shard_map/psum | solution.py:30
  489.6 2.6 multiply_reduce_fusion
  492.3 7.4 %fusion.40 = bf16[128,1344]{0,1:T(8,128)(2,1)S(1)} fusion(bf16[1,1344,5280]{2,1,0:T(8,128)(2,1)} %copy-done.2, bf16[128,5280]{0,1:T(8,128)(2,1)S(1)} %copy-done.8, bf16[128,5280]{0,1:T(8,128)(2,1)S(1)} %copy-done.6, f32[128]{0:T(128)S(1)} %add_rsqrt_fusion), kind=kOutput, calls=%fused_computation.43 | convolution fusion | flops 1820209152 | bytes 17240576 | tf_op jit(solution)/shard_map/dot_general | solution.py:34
  499.7 3.7 collective-permute-start.8
  503.4 2.6 collective-permute-start.9
  505.9 3.4 collective-permute-start.10
  509.3 14.1 %collective-permute-start.11 = (bf16[128,1344]{0,1:T(8,128)(2,1)S(1)}, bf16[128,1344]{0,1:T(8,128)(2,1)S(1)}, u32[]{:S(2)}, u32[]{:S(2)}) collective-permute-start(bf16[128,1344]{0,1:T(8,128)(2,1)S(1)} %fusion.40), channel_id=1, source_target_pairs={{0,2},{2,4},{4,6},{6,8},{8,10},{10,12},{12,14},{14,16},{16,18},{18... | collective-permute-start | bytes 1032200 | tf_op jit(solution)/shard_map/ppermute | solution.py:20
  524.3 4.1 fusion.46
  529.6 1.3 collective-permute-start.19
  530.9 1.3 collective-permute-start.18
  532.3 1.3 collective-permute-start.17
  533.7 1.3 collective-permute-start.16
  536.0 10.8 %fusion.26 = bf16[128,5280]{0,1:T(8,128)(2,1)} fusion(bf16[128,1344]{0,1:T(8,128)(2,1)S(1)} %bitcast.98, bf16[1,1344,5280]{2,1,0:T(8,128)(2,1)} %copy-done.3), kind=kOutput, calls=%fused_computation.20 | convolution fusion | flops 1817333760 | bytes 15888384 | tf_op jit(solution)/shard_map/dot_general | solution.py:109
  546.8 10.8 %fusion.20 = bf16[128,5280]{0,1:T(8,128)(2,1)} fusion(bf16[1,1344,5280]{2,1,0:T(8,128)(2,1)} %copy-done.2, bf16[128,1344]{0,1:T(8,128)(2,1)S(1)} %bitcast.96, bf16[128,1344]{0,1:T(8,128)(2,1)S(1)} %collective-permute-done.19, bf16[128,1344]{0,1:T(8,128)(2,1)S(1)} %collective-permute-done.18, bf16[128,1344]{0,1:T(8,128)(2,1)S(1)} %collective-permute-done.17, ...), kind=kOutput, calls=%fused_computation.18 | convolution fusion | flops 1819054080 | bytes 17264640 | tf_op jit(solution)/shard_map/dot_general | solution.py:132
  557.7 88.0 %all-reduce.6.cloned.1.call-done = (bf16[128,5280]{0,1:T(8,128)(2,1)}, bf16[128,5280]{0,1:T(8,128)(2,1)}) async-done(((bf16[128,5280]{0,1:T(8,128)(2,1)}, bf16[128,5280]{0,1:T(8,128)(2,1)}), (bf16[128,5280]{0,1:T(8,128)(2,1)}, bf16[128,5280]{0,1:T(8,128)(2,1)})) %all-reduce.6.cloned.1.call-update) | async-done | bytes 2703376 | tf_op jit(solution)/shard_map/psum | solution.py:30
  645.7 2.2 fusion.38
  647.9 5.8 fusion.37
  (99 shorter events, 12.8 us)
Async XLA Ops:
  7.2 46.1 %copy-start = (bf16[128,1344]{0,1:T(8,128)(2,1)S(1)}, bf16[128,1344]{0,1:T(8,128)(2,1)}, u32[]{:S(2)}) copy-start(bf16[128,1344]{0,1:T(8,128)(2,1)} %param.8) | copy-start | bytes 1032196
  7.2 4.1 copy-start.14
  7.2 163.6 %all-gather.3.cloned.1.call-start = ((), (), s32[]{:S(2)}) async-start(), calls=%async_computation | async-start | bytes 30707712 | tf_op jit(solution)/shard_map/all_gather | solution.py:70
  11.2 2.8 copy-start.15
  11.2 16.4 %copy-start.17 = (s32[16]{0:T(128)S(1)}, s32[16]{0:T(128)}, u32[]{:S(2)}) copy-start(s32[16]{0:T(128)} %param.12) | copy-start | bytes 196
  11.2 18.1 %copy-start.4 = (bf16[128,5280]{0,1:T(8,128)(2,1)S(1)}, bf16[128,5280]{0,1:T(8,128)(2,1)}, u32[]{:S(2)}) copy-start(bf16[128,5280]{0,1:T(8,128)(2,1)} %param.7) | copy-start | bytes 4055044
  11.2 331.6 %all-gather.5.cloned.1.call-start = ((), (), s32[]{:S(2)}) async-start(), calls=%async_computation.1 | async-start | bytes 30707712 | tf_op jit(solution)/shard_map/all_gather | solution.py:71
  13.9 475.7 %all-reduce.8.cloned.1.call-start = ((), (), s32[]{:S(2)}) async-start(), calls=%async_computation.3 | async-start | bytes 5406720 | tf_op jit(solution)/shard_map/psum | solution.py:30
  14.0 20.4 %collective-permute-start.4 = (bf16[128,1344]{0,1:T(8,128)(2,1)S(1)}, bf16[128,1344]{0,1:T(8,128)(2,1)}, u32[]{:S(2)}, u32[]{:S(2)}) collective-permute-start(bf16[128,1344]{0,1:T(8,128)(2,1)S(1)} %copy-done.15), channel_id=1, source_target_pairs={{0,8},{2,10},{4,12},{6,14},{8,16},{10,18},{12,20},{14,22},{16,24},... | collective-permute-start | bytes 1032200 | tf_op jit(solution)/shard_map/ppermute | solution.py:20
  19.6 17.4 %collective-permute-start.5 = (bf16[128,1344]{0,1:T(8,128)(2,1)S(1)}, bf16[128,1344]{0,1:T(8,128)(2,1)S(1)}, u32[]{:S(2)}, u32[]{:S(2)}) collective-permute-start(bf16[128,1344]{0,1:T(8,128)(2,1)S(1)} %copy-done.15), channel_id=1, source_target_pairs={{0,6},{2,8},{4,10},{6,12},{8,14},{10,16},{12,18},{14,20},{16,22},{... | collective-permute-start | bytes 1032200 | tf_op jit(solution)/shard_map/ppermute | solution.py:20
  22.2 29.6 %collective-permute-start.6 = (bf16[128,1344]{0,1:T(8,128)(2,1)S(1)}, bf16[128,1344]{0,1:T(8,128)(2,1)S(1)}, u32[]{:S(2)}, u32[]{:S(2)}) collective-permute-start(bf16[128,1344]{0,1:T(8,128)(2,1)S(1)} %copy-done.15), channel_id=1, source_target_pairs={{0,4},{2,6},{4,8},{6,10},{8,12},{10,14},{12,16},{14,18},{16,20},{1... | collective-permute-start | bytes 1032200 | tf_op jit(solution)/shard_map/ppermute | solution.py:20
  25.0 26.9 %collective-permute-start.7 = (bf16[128,1344]{0,1:T(8,128)(2,1)S(1)}, bf16[128,1344]{0,1:T(8,128)(2,1)S(1)}, u32[]{:S(2)}, u32[]{:S(2)}) collective-permute-start(bf16[128,1344]{0,1:T(8,128)(2,1)S(1)} %copy-done.15), channel_id=1, source_target_pairs={{0,2},{2,4},{4,6},{6,8},{8,10},{10,12},{12,14},{14,16},{16,18},{18... | collective-permute-start | bytes 1032200 | tf_op jit(solution)/shard_map/ppermute | solution.py:20
  52.1 1.2 copy-start.16
  170.8 13.9 %copy-start.5 = (bf16[128,5280]{0,1:T(8,128)(2,1)S(1)}, bf16[128,5280]{0,1:T(8,128)(2,1)}, u32[]{:S(2)}) copy-start(bf16[128,5280]{0,1:T(8,128)(2,1)} %param.7) | copy-start | bytes 4055044
  184.7 5.1 copy-start.2
  189.8 174.6 %collective-permute-start = (bf16[128,1344]{0,1:T(8,128)(2,1)S(1)}, bf16[128,1344]{0,1:T(8,128)(2,1)}, u32[]{:S(2)}, u32[]{:S(2)}) collective-permute-start(bf16[128,1344]{0,1:T(8,128)(2,1)S(1)} %fusion.43), channel_id=1, source_target_pairs={{0,8},{2,10},{4,12},{6,14},{8,16},{10,18},{12,20},{14,22},{16,24},... | collective-permute-start | bytes 1032200 | tf_op jit(solution)/shard_map/ppermute | solution.py:20
  192.1 174.7 %collective-permute-start.1 = (bf16[128,1344]{0,1:T(8,128)(2,1)S(1)}, bf16[128,1344]{0,1:T(8,128)(2,1)}, u32[]{:S(2)}, u32[]{:S(2)}) collective-permute-start(bf16[128,1344]{0,1:T(8,128)(2,1)S(1)} %fusion.43), channel_id=1, source_target_pairs={{0,6},{2,8},{4,10},{6,12},{8,14},{10,16},{12,18},{14,20},{16,22},{... | collective-permute-start | bytes 1032200 | tf_op jit(solution)/shard_map/ppermute | solution.py:20
  210.9 158.2 %collective-permute-start.2 = (bf16[128,1344]{0,1:T(8,128)(2,1)S(1)}, bf16[128,1344]{0,1:T(8,128)(2,1)S(1)}, u32[]{:S(2)}, u32[]{:S(2)}) collective-permute-start(bf16[128,1344]{0,1:T(8,128)(2,1)S(1)} %fusion.43), channel_id=1, source_target_pairs={{0,4},{2,6},{4,8},{6,10},{8,12},{10,14},{12,16},{14,18},{16,20},{1... | collective-permute-start | bytes 1032200 | tf_op jit(solution)/shard_map/ppermute | solution.py:20
  212.7 157.9 %collective-permute-start.3 = (bf16[128,1344]{0,1:T(8,128)(2,1)S(1)}, bf16[128,1344]{0,1:T(8,128)(2,1)S(1)}, u32[]{:S(2)}, u32[]{:S(2)}) collective-permute-start(bf16[128,1344]{0,1:T(8,128)(2,1)S(1)} %fusion.43), channel_id=1, source_target_pairs={{0,2},{2,4},{4,6},{6,8},{8,10},{10,12},{12,14},{14,16},{16,18},{18... | collective-permute-start | bytes 1032200 | tf_op jit(solution)/shard_map/ppermute | solution.py:20
  342.8 13.9 %copy-start.11 = (bf16[128,5280]{0,1:T(8,128)(2,1)S(1)}, bf16[128,5280]{0,1:T(8,128)(2,1)}, u32[]{:S(2)}) copy-start(bf16[128,5280]{0,1:T(8,128)(2,1)} %param.13) | copy-start | bytes 4055044
  356.7 5.1 copy-start.3
  363.1 19.1 %collective-permute-start.15 = (bf16[128,1344]{0,1:T(8,128)(2,1)S(1)}, bf16[128,1344]{0,1:T(8,128)(2,1)S(1)}, u32[]{:S(2)}, u32[]{:S(2)}) collective-permute-start(bf16[128,1344]{0,1:T(8,128)(2,1)S(1)} %bitcast.107), channel_id=1, source_target_pairs={{8,0},{10,2},{12,4},{14,6},{16,8},{18,10},{20,12},{22,14},{24,16},... | collective-permute-start | bytes 1032200 | tf_op jit(solution)/shard_map/ppermute | solution.py:20
  364.5 19.5 %collective-permute-start.14 = (bf16[128,1344]{0,1:T(8,128)(2,1)S(1)}, bf16[128,1344]{0,1:T(8,128)(2,1)S(1)}, u32[]{:S(2)}, u32[]{:S(2)}) collective-permute-start(bf16[128,1344]{0,1:T(8,128)(2,1)S(1)} %bitcast.105), channel_id=1, source_target_pairs={{6,0},{8,2},{10,4},{12,6},{14,8},{16,10},{18,12},{20,14},{22,16},{... | collective-permute-start | bytes 1032200 | tf_op jit(solution)/shard_map/ppermute | solution.py:20
  366.8 23.6 %collective-permute-start.13 = (bf16[128,1344]{0,1:T(8,128)(2,1)S(1)}, bf16[128,1344]{0,1:T(8,128)(2,1)S(1)}, u32[]{:S(2)}, u32[]{:S(2)}) collective-permute-start(bf16[128,1344]{0,1:T(8,128)(2,1)S(1)} %bitcast.103), channel_id=1, source_target_pairs={{4,0},{6,2},{8,4},{10,6},{12,8},{14,10},{16,12},{18,14},{20,16},{2... | collective-permute-start | bytes 1032200 | tf_op jit(solution)/shard_map/ppermute | solution.py:20
  369.2 21.3 %collective-permute-start.12 = (bf16[128,1344]{0,1:T(8,128)(2,1)S(1)}, bf16[128,1344]{0,1:T(8,128)(2,1)S(1)}, u32[]{:S(2)}, u32[]{:S(2)}) collective-permute-start(bf16[128,1344]{0,1:T(8,128)(2,1)S(1)} %bitcast.101), channel_id=1, source_target_pairs={{2,0},{4,2},{6,4},{8,6},{10,8},{12,10},{14,12},{16,14},{18,16},{20... | collective-permute-start | bytes 1032200 | tf_op jit(solution)/shard_map/ppermute | solution.py:20
  401.3 244.4 %all-reduce.6.cloned.1.call-start = ((), (), s32[]{:S(2)}) async-start(), calls=%async_computation.2 | async-start | bytes 5406720 | tf_op jit(solution)/shard_map/psum | solution.py:30
  489.6 2.6 copy-start.6
  489.6 2.6 copy-start.8
  492.2 32.0 %slice-start = ((s8[14450688]{0:T(1024)(128)(4,1)}), s8[4194304]{0:T(1024)(128)(4,1)S(1)}, s32[]{:S(2)}) async-start(s8[14450688]{0:T(1024)(128)(4,1)} %bitcast.92), calls=%async_computation.4 | async-start | bytes 8388608
  492.2 31.2 %copy-start.9 = (bf16[128,5280]{0,1:T(8,128)(2,1)S(1)}, bf16[128,5280]{0,1:T(8,128)(2,1)}, u32[]{:S(2)}) copy-start(bf16[128,5280]{0,1:T(8,128)(2,1)} %get-tuple-element.5) | copy-start | bytes 4055044
  492.2 32.0 %slice-start.1 = ((s8[14450688]{0:T(1024)(128)(4,1)}), s8[4194304]{0:T(1024)(128)(4,1)S(1)}, s32[]{:S(2)}) async-start(s8[14450688]{0:T(1024)(128)(4,1)} %bitcast.92), calls=%async_computation.5 | async-start | bytes 8388608
  492.2 32.0 %slice-start.2 = ((s8[14450688]{0:T(1024)(128)(4,1)}), s8[4194304]{0:T(1024)(128)(4,1)S(1)}, s32[]{:S(2)}) async-start(s8[14450688]{0:T(1024)(128)(4,1)} %bitcast.92), calls=%async_computation.6 | async-start | bytes 8388608
  492.2 32.0 %slice-start.3 = ((s8[14450688]{0:T(1024)(128)(4,1)}), s8[1867776]{0:T(1024)(128)(4,1)S(1)}, s32[]{:S(2)}) async-start(s8[14450688]{0:T(1024)(128)(4,1)} %bitcast.92), calls=%async_computation.7 | async-start | bytes 3735552
  499.7 24.6 %copy-start.12 = (bf16[128,5280]{0,1:T(8,128)(2,1)S(1)}, bf16[128,5280]{0,1:T(8,128)(2,1)}, u32[]{:S(2)}) copy-start(bf16[128,5280]{0,1:T(8,128)(2,1)} %param.13) | copy-start | bytes 4055044
  499.7 31.2 %collective-permute-start.8 = (bf16[128,1344]{0,1:T(8,128)(2,1)S(1)}, bf16[128,1344]{0,1:T(8,128)(2,1)S(1)}, u32[]{:S(2)}, u32[]{:S(2)}) collective-permute-start(bf16[128,1344]{0,1:T(8,128)(2,1)S(1)} %fusion.40), channel_id=1, source_target_pairs={{0,8},{2,10},{4,12},{6,14},{8,16},{10,18},{12,20},{14,22},{16,24},... | collective-permute-start | bytes 1032200 | tf_op jit(solution)/shard_map/ppermute | solution.py:20
  503.4 28.9 %collective-permute-start.9 = (bf16[128,1344]{0,1:T(8,128)(2,1)S(1)}, bf16[128,1344]{0,1:T(8,128)(2,1)S(1)}, u32[]{:S(2)}, u32[]{:S(2)}) collective-permute-start(bf16[128,1344]{0,1:T(8,128)(2,1)S(1)} %fusion.40), channel_id=1, source_target_pairs={{0,6},{2,8},{4,10},{6,12},{8,14},{10,16},{12,18},{14,20},{16,22},{... | collective-permute-start | bytes 1032200 | tf_op jit(solution)/shard_map/ppermute | solution.py:20
  505.9 27.8 %collective-permute-start.10 = (bf16[128,1344]{0,1:T(8,128)(2,1)S(1)}, bf16[128,1344]{0,1:T(8,128)(2,1)S(1)}, u32[]{:S(2)}, u32[]{:S(2)}) collective-permute-start(bf16[128,1344]{0,1:T(8,128)(2,1)S(1)} %fusion.40), channel_id=1, source_target_pairs={{0,4},{2,6},{4,8},{6,10},{8,12},{10,14},{12,16},{14,18},{16,20},{1... | collective-permute-start | bytes 1032200 | tf_op jit(solution)/shard_map/ppermute | solution.py:20
  509.3 25.8 %collective-permute-start.11 = (bf16[128,1344]{0,1:T(8,128)(2,1)S(1)}, bf16[128,1344]{0,1:T(8,128)(2,1)S(1)}, u32[]{:S(2)}, u32[]{:S(2)}) collective-permute-start(bf16[128,1344]{0,1:T(8,128)(2,1)S(1)} %fusion.40), channel_id=1, source_target_pairs={{0,2},{2,4},{4,6},{6,8},{8,10},{10,12},{12,14},{14,16},{16,18},{18... | collective-permute-start | bytes 1032200 | tf_op jit(solution)/shard_map/ppermute | solution.py:20
  529.6 17.2 %collective-permute-start.19 = (bf16[128,1344]{0,1:T(8,128)(2,1)S(1)}, bf16[128,1344]{0,1:T(8,128)(2,1)S(1)}, u32[]{:S(2)}, u32[]{:S(2)}) collective-permute-start(bf16[128,1344]{0,1:T(8,128)(2,1)S(1)} %bitcast.106), channel_id=1, source_target_pairs={{8,0},{10,2},{12,4},{14,6},{16,8},{18,10},{20,12},{22,14},{24,16},... | collective-permute-start | bytes 1032200 | tf_op jit(solution)/shard_map/ppermute | solution.py:20
  530.9 15.9 %collective-permute-start.18 = (bf16[128,1344]{0,1:T(8,128)(2,1)S(1)}, bf16[128,1344]{0,1:T(8,128)(2,1)S(1)}, u32[]{:S(2)}, u32[]{:S(2)}) collective-permute-start(bf16[128,1344]{0,1:T(8,128)(2,1)S(1)} %bitcast.104), channel_id=1, source_target_pairs={{6,0},{8,2},{10,4},{12,6},{14,8},{16,10},{18,12},{20,14},{22,16},{... | collective-permute-start | bytes 1032200 | tf_op jit(solution)/shard_map/ppermute | solution.py:20
  532.3 14.5 %collective-permute-start.17 = (bf16[128,1344]{0,1:T(8,128)(2,1)S(1)}, bf16[128,1344]{0,1:T(8,128)(2,1)S(1)}, u32[]{:S(2)}, u32[]{:S(2)}) collective-permute-start(bf16[128,1344]{0,1:T(8,128)(2,1)S(1)} %bitcast.102), channel_id=1, source_target_pairs={{4,0},{6,2},{8,4},{10,6},{12,8},{14,10},{16,12},{18,14},{20,16},{2... | collective-permute-start | bytes 1032200 | tf_op jit(solution)/shard_map/ppermute | solution.py:20
  533.7 13.1 %collective-permute-start.16 = (bf16[128,1344]{0,1:T(8,128)(2,1)S(1)}, bf16[128,1344]{0,1:T(8,128)(2,1)S(1)}, u32[]{:S(2)}, u32[]{:S(2)}) collective-permute-start(bf16[128,1344]{0,1:T(8,128)(2,1)S(1)} %bitcast.100), channel_id=1, source_target_pairs={{2,0},{4,2},{6,4},{8,6},{10,8},{12,10},{14,12},{16,14},{18,16},{20... | collective-permute-start | bytes 1032200 | tf_op jit(solution)/shard_map/ppermute | solution.py:20
  557.6 88.1 %copy-start.7 = (bf16[128,5280]{0,1:T(8,128)(2,1)S(1)}, bf16[128,5280]{0,1:T(8,128)(2,1)}, u32[]{:S(2)}) copy-start(bf16[128,5280]{0,1:T(8,128)(2,1)} %param.7) | copy-start | bytes 4055044
  645.7 2.2 copy-start.10
  645.7 2.2 copy-start.13
  647.9 5.8 copy-start.1
Sparse Core Ops, SparseCore 0:
  11.3 159.4 all-gather.2
  172.3 170.4 all-gather.4
  401.4 88.1 all-reduce.7
  557.8 87.8 all-reduce.5
where the time goes:
time: 664 us; the launch traced here: 660 us
  waiting for transfers between devices  442 us (67%)
  starting transfers between devices  73.2 us (11%)
  matrix products  71.5 us (11%)
  local copies, waits for them, and re-layouts  43.5 us (7%)
  other arithmetic  15.9 us (2%)
  between operations  14.6 us (2%)
    psum x2, waiting for transfers between devices, head_total(): lax.psum(partial_value.astype(jnp.bfloat16), 'fsdp').astype(jnp.float32)  176 us
    all_gather x1, waiting for transfers between devices, local(): lax.all_gather(out_weight, 'seq', axis=1, tiled=True)  128 us
    all_gather x1, waiting for transfers between devices, local(): lax.all_gather(value_weight, 'seq', axis=1, tiled=True)  109 us
    ppermute x20, starting transfers between devices, from_behind(): lax.ppermute(value, axis, [(source, source + steps) for source in range(f...  73 us
    unnamed x60, local copies, waits for them, and re-layouts  41.8 us
    ppermute x20, waiting for transfers between devices, from_behind(): lax.ppermute(value, axis, [(source, source + steps) for source in range(f...  28.9 us
    dot_general x2, matrix products, local(): jnp.dot(dvalues, value_rows, preferred_element_type=jnp.float32)  21.6 us
    dot_general x2, matrix products, local(): jnp.dot(attended, out_rows, preferred_element_type=jnp.float32)  21.6 us
  transfers between devices with their start and end apart: 24, of which 9 were waited for; matrix products, arithmetic and copies ran while one was open for 13% of the time, Pallas kernels for 0%

commit v1 on v0

--- a/solution.py
+++ b/solution.py
@@ -1,14 +1,19 @@
+import functools
 import math
 
 import jax
 import jax.numpy as jnp
 from jax import lax
+from jax.experimental import pallas as pl
+from jax.experimental.pallas import tpu as pltpu
 from jax.sharding import PartitionSpec as P
 
 HEAD_DIM = 96
 BLOCK = 128
 UNROLL = 2
 REACH = 4
+PLANE = 4
+MESH = pl.DeviceIdType.MESH
 
 
 epsilon = 1e-06
@@ -27,13 +32,176 @@
 
 
 def head_total(partial_value):
-    return lax.psum(partial_value.astype(jnp.bfloat16), "fsdp").astype(jnp.float32)
+    own = partial_value.astype(jnp.bfloat16)
+    if lax.axis_size("fsdp") != 2:
+        return lax.psum(own, "fsdp").astype(jnp.float32)
+    other = lax.ppermute(own, "fsdp", [(0, 1), (1, 0)])
+    return own.astype(jnp.float32) + other.astype(jnp.float32)
 
 
 def contract_last(left, right):
     return lax.dot_general(
         left, right, (((1,), (1,)), ((), ())), preferred_element_type=jnp.float32
     )
+
+
+def gather_kernel(
+    lines, wv_ref, wo_ref, full_v, full_o, slots_v, slots_o,
+    raw, packed, own_sem, send_z, recv_z, send_x, recv_x, send_c, recv_c, load_sem, store_sem,
+):
+    me = lax.axis_index("seq")
+    group = lax.axis_index("fsdp")
+    line, inner = me // PLANE, me % PLANE
+    side, core = inner // 2, inner % 2
+    rows, width = wv_ref.shape
+    shards, slots, fulls = (wv_ref, wo_ref), (slots_v, slots_o), (full_v, full_o)
+
+    def device(other_line, other_side, other_core):
+        return (other_line * PLANE + other_side * 2 + other_core, group)
+
+    right, left = device(line + 1, side, core), device(line - 1, side, core)
+    across, twin = device(line, 1 - side, core), device(line, side, 1 - core)
+    has_right, has_left = line + 1 < lines, line >= 1
+
+    own = [pltpu.make_async_copy(shards[w], slots[w].at[me], own_sem.at[w]) for w in range(2)]
+    for copy in own:
+        copy.start()
+    barrier = pltpu.get_barrier_semaphore()
+    for there in (across, twin):
+        pl.semaphore_signal(barrier, inc=1, device_id=there, device_id_type=MESH)
+    for exists, there in ((has_right, right), (has_left, left)):
+        @pl.when(exists)
+        def _():
+            pl.semaphore_signal(barrier, inc=1, device_id=there, device_id_type=MESH)
+    neighbours = 2 + has_right.astype(jnp.int32) + has_left.astype(jnp.int32)
+    pl.semaphore_wait(barrier, neighbours)
+    for copy in own:
+        copy.wait()
+
+    def along(w, origin, way):
+        slot = slots[w].at[origin * PLANE + inner]
+        return pltpu.make_async_remote_copy(
+            src_ref=slot, dst_ref=slot, send_sem=send_z.at[w, way, origin],
+            recv_sem=recv_z.at[w, origin], device_id=right if way == 0 else left, device_id_type=MESH)
+
+    def crossing(w, origin, to_me=False):
+        slot = slots[w].at[origin * PLANE + ((1 - side) if to_me else side) * 2 + core]
+        return pltpu.make_async_remote_copy(
+            src_ref=slot, dst_ref=slot, send_sem=send_x.at[w, origin],
+            recv_sem=recv_x.at[w, origin], device_id=across, device_id_type=MESH)
+
+    def twinned(w, origin, far, to_me=False):
+        which = (1 - side) if far else side
+        slot = slots[w].at[origin * PLANE + which * 2 + ((1 - core) if to_me else core)]
+        return pltpu.make_async_remote_copy(
+            src_ref=slot, dst_ref=slot, send_sem=send_c.at[w, origin, far],
+            recv_sem=recv_c.at[w, origin, far], device_id=twin, device_id_type=MESH)
+
+    def arrived(w, origin):
+        crossing(w, origin).start()
+        twinned(w, origin, 0).start()
+
+    def crossed(w, origin):
+        crossing(w, origin, True).wait_recv()
+        twinned(w, origin, 1).start()
+
+    def pack(w, origin):
+        for far in range(2):
+            twinned(w, origin, far, True).wait_recv()
+        loads = [
+            pltpu.make_async_copy(slots[w].at[origin * PLANE + k], raw.at[k], load_sem.at[k])
+            for k in range(PLANE)
+        ]
+        for copy in loads:
+            copy.start()
+        for copy in loads:
+            copy.wait()
+        for low in range(0, width, 384):
+            high = min(low + 384, width)
+            for k in range(PLANE):
+                packed[k * rows:(k + 1) * rows, low:high] = raw[k, :, low:high]
+        store = pltpu.make_async_copy(packed, fulls[w].at[origin], store_sem)
+        store.start()
+        store.wait()
+
+    def forward(w, step):
+        for way in range(2):
+            origin = line - step if way == 0 else line + step
+
+            @pl.when((origin >= 0) if way == 0 else (origin < lines))
+            def _():
+                along(w, origin, way).wait_recv()
+
+                @pl.when(has_right if way == 0 else has_left)
+                def _():
+                    along(w, origin, way).start()
+                arrived(w, origin)
+
+    def each(step, act):
+        if step == 0:
+            act(line)
+            return
+        for origin, exists in ((line - step, line >= step), (line + step, line + step < lines)):
+            pl.when(exists)(functools.partial(act, origin))
+
+    for w in range(2):
+        for exists, way in ((has_right, 0), (has_left, 1)):
+            @pl.when(exists)
+            def _():
+                along(w, line, way).start()
+        arrived(w, line)
+    order = [(step, w) for step in range(lines) for w in range(2)]
+    count = len(order)
+    for turn in range(2, count + 3):
+        if turn < count:
+            forward(order[turn][1], order[turn][0])
+        if 0 <= turn - 2 < count:
+            step, w = order[turn - 2]
+            each(step, functools.partial(crossed, w))
+        if 0 <= turn - 3 < count:
+            step, w = order[turn - 3]
+            each(step, functools.partial(pack, w))
+    for w in range(2):
+        for origin in range(lines):
+            crossing(w, origin).wait_send()
+            for far in range(2):
+                twinned(w, origin, far).wait_send()
+        for step in range(lines):
+            pl.when(has_right & (line >= step))(lambda: along(w, line - step, 0).wait_send())
+            pl.when(has_left & (line + step < lines))(lambda: along(w, line + step, 1).wait_send())
+
+
+def gather_rows(value_weight, out_weight):
+    count = lax.axis_size("seq")
+    rows, width = value_weight.shape[1:]
+    lines = count // PLANE
+    if count % PLANE or (PLANE * rows) % 16 or rows % 2:
+        return tuple(
+            lax.all_gather(weight, "seq", axis=1, tiled=True)[0]
+            for weight in (value_weight, out_weight)
+        )
+    full = jax.ShapeDtypeStruct((lines, PLANE * rows, width), jnp.bfloat16)
+    slot = jax.ShapeDtypeStruct((count, rows, width), jnp.bfloat16)
+    dma = pltpu.SemaphoreType.DMA
+    full_v, full_o, _, _ = pl.pallas_call(
+        functools.partial(gather_kernel, lines),
+        out_shape=(full, full, slot, slot),
+        in_specs=[pl.BlockSpec(memory_space=pl.ANY)] * 2,
+        out_specs=[pl.BlockSpec(memory_space=pl.ANY)] * 4,
+        scratch_shapes=[
+            pltpu.VMEM((PLANE, rows, width), jnp.bfloat16),
+            pltpu.VMEM((PLANE * rows, width), jnp.bfloat16),
+            dma((2,)),
+            dma((2, 2, lines)), dma((2, lines)),
+            dma((2, lines)), dma((2, lines)),
+            dma((2, lines, 2)), dma((2, lines, 2)),
+            dma((PLANE,)), dma,
+        ],
+        compiler_params=pltpu.CompilerParams(
+            collective_id=0, has_side_effects=True, vmem_limit_bytes=40 * 1024 * 1024
+        ),
+    )(value_weight[0], out_weight[0])
+    return full_v.reshape(count * rows, width), full_o.reshape(count * rows, width)
 
 
 def fetch_first(pair):
@@ -66,12 +234,7 @@
     allowed = (key_docs[None, :] == query_docs[:, None]) & (
         slot_rows[None, :] <= query_rows[:, None]
     )
-    gathered_value, gathered_out = (
-        lax.all_gather(value_weight, "seq", axis=1, tiled=True),
-        lax.all_gather(out_weight, "seq", axis=1, tiled=True),
-    )
-    value_rows = gathered_value[0]
-    out_rows = gathered_out[0]
+    value_rows, out_rows = gather_rows(value_weight, out_weight)
     current = state_in.astype(jnp.float32)
     records = []
     soft_weights = None

time: 664 us -> 468 us (0.70)
  waiting for transfers between devices: 442 us -> 113 us
  Pallas kernels: 0 us -> 177 us
  local copies, waits for them, and re-layouts: 43.5 us -> 17.2 us
  starting transfers between devices: 73.2 us -> 48.7 us
  matrix products: 71.5 us -> 85.8 us
  between operations: 14.6 us -> 1.71 us
    all_gather x2 -> x0, waiting for transfers between devices: 237 us -> none  [the longest x1 128 us: local(): lax.all_gather(out_weight, 'seq', axis=1, tiled=True)]
    pallas_call x0 -> x1, Pallas kernels: none -> 177 us  [gather_rows(): pl.pallas_call(functools.partial(gather_kernel, lines), out_shape=(full,...]
    psum x2 -> x0, waiting for transfers between devices: 176 us -> none  [head_total(): lax.psum(partial_value.astype(jnp.bfloat16), 'fsdp').astype(jnp.float32)]
    ppermute x0 -> x4, waiting for transfers between devices: none -> 51.7 us  [head_total(): other = lax.ppermute(own, 'fsdp', [(0, 1), (1, 0)])]
    ppermute x20, waiting for transfers between devices: 28.9 us -> 61.4 us  [from_behind(): lax.ppermute(value, axis, [(source, source + steps) for source in range(f...]
    ppermute x20, starting transfers between devices: 73 us -> 44.5 us  [from_behind(): lax.ppermute(value, axis, [(source, source + steps) for source in range(f...]
    unnamed x60 -> x68, local copies, waits for them, and re-layouts: 41.8 us -> 13.9 us
    dot_general x4, matrix products: 19.4 us -> 31 us  [contract_last(): lax.dot_general(left, right, (((1,), (1,)), ((), ())), preferred_element_...]
  transfers between devices with their start and end apart: 24 -> 24, of which waited for: 9 -> 9; matrix products, arithmetic and copies ran while one was open for 13% -> 15% of each run, Pallas kernels for 0% -> 0%
where the time goes in v1:
time: 468 us; the launch traced here: 460 us
  Pallas kernels  177 us (38%)
  waiting for transfers between devices  113 us (24%)
  matrix products  85.8 us (18%)
  starting transfers between devices  48.7 us (10%)
  local copies, waits for them, and re-layouts  17.2 us (4%)
  other arithmetic  16.4 us (4%)
    pallas_call x1, Pallas kernels, gather_rows(): pl.pallas_call(functools.partial(gather_kernel, lines), out_shape=(full,...  177 us
    ppermute x20, waiting for transfers between devices, from_behind(): lax.ppermute(value, axis, [(source, source + steps) for source in range(f...  61.4 us
    ppermute x4, waiting for transfers between devices, head_total(): other = lax.ppermute(own, 'fsdp', [(0, 1), (1, 0)])  51.7 us
    ppermute x20, starting transfers between devices, from_behind(): lax.ppermute(value, axis, [(source, source + steps) for source in range(f...  44.5 us
    dot_general x4, matrix products, contract_last(): lax.dot_general(left, right, (((1,), (1,)), ((), ())), preferred_element_...  31 us
    dot_general x2, matrix products, local(): jnp.dot(dvalues, value_rows, preferred_element_type=jnp.float32)  22.8 us
    dot_general x2, matrix products, local(): jnp.dot(attended, out_rows, preferred_element_type=jnp.float32)  20.8 us
    unnamed x68, local copies, waits for them, and re-layouts  13.9 us
  transfers between devices with their start and end apart: 24, of which 9 were waited for; matrix products, arithmetic and copies ran while one was open for 15% of the time, Pallas kernels for 0%

profile of v1, /device:TPU:0, one launch (start us, length us, event | category | flops | bytes accessed | tf_op | source)
XLA Modules:
  0.0 459.7 jit_solution(8262084969465982192)
XLA Ops:
  0.7 2.2 fusion.9
  5.2 176.8 %shard_map.86 = (bf16[4,336,5280]{2,1,0:T(8,128)(2,1)}, bf16[4,336,5280]{2,1,0:T(8,128)(2,1)}, bf16[16,84,5280]{2,1,0:T(8,128)(2,1)}, bf16[16,84,5280]{2,1,0:T(8,128)(2,1)}) custom-call(bf16[84,5280]{1,0:T(8,128)(2,1)S(1)} %bitcast.72, bf16[84,5280]{1,0:T(8,128)(2,1)S(1)} %bitcast.73), custom_call_target="tpu_custom_call" | custom-call | tf_op jit(solution)/shard_map/pallas_call | solution.py:186
  182.1 8.0 %convolution_convert_fusion.6 = bf16[128,1344]{0,1:T(8,128)(2,1)} fusion(bf16[1344,5280]{1,0:T(8,128)(2,1)} %bitcast.80, bf16[128,5280]{0,1:T(8,128)(2,1)S(1)} %copy-done.4, f32[128]{0:T(128)S(1)} %add_rsqrt_fusion.1), kind=kOutput, calls=%fused_computation.28 | convolution fusion | flops 1818857472 | bytes 15888896 | tf_op jit(solution)/shard_map/dot_general | solution.py:43
  190.1 4.3 collective-permute-start
  194.4 2.0 collective-permute-start.1
  196.4 3.9 collective-permute-start.2
  200.3 2.5 collective-permute-start.3
  202.8 3.2 collective-permute-start.4
  207.5 7.9 %convolution_convert_fusion.7 = bf16[1344,128]{1,0:T(8,128)(2,1)} fusion(bf16[1344,5280]{1,0:T(8,128)(2,1)} %bitcast.74, bf16[128,5280]{0,1:T(8,128)(2,1)S(1)} %copy-done.9), kind=kOutput, calls=%fused_computation.29 | convolution fusion | flops 1816829952 | bytes 15888384 | tf_op jit(solution)/shard_map/dot_general | solution.py:43
  215.7 3.0 collective-permute-start.5
  218.7 1.8 constant_dynamic-update-slice_fusion.4
  220.4 2.4 collective-permute-start.6
  222.8 1.8 constant_dynamic-update-slice_fusion.3
  224.6 1.6 collective-permute-start.7
  226.2 1.8 constant_dynamic-update-slice_fusion.2
  228.0 1.8 constant_dynamic-update-slice_fusion.1
  229.8 1.8 constant_dynamic-update-slice_fusion
  234.2 5.6 %fusion.36 = (f32[14,128]{1,0:T(8,128)S(1)}, f32[14,128,640]{1,2,0:T(8,128)}) fusion(pred[128,640]{0,1:T(8,128)(4,1)S(1)} %fusion.29, bf16[640,14,96]{0,2,1:T(8,128)(2,1)} %bitcast.99, bf16[128,14,96]{0,2,1:T(8,128)(2,1)S(1)} %bitcast.71), kind=kOutput, calls=%fused_computation.83 | convolution fusion | flops 225936000 | bytes 6740992 | tf_op jit(solution)/shard_map/sub | solution.py:258
  239.8 2.8 divide_convert_fusion
  242.7 2.2 convolution_convert_fusion.11
  244.8 9.8 %convolution_convert_fusion.3 = bf16[128,5280]{0,1:T(8,128)(2,1)S(1)} fusion(bf16[128,1344]{0,1:T(8,128)(2,1)S(1)} %bitcast.88, bf16[1344,5280]{1,0:T(8,128)(2,1)} %bitcast.75), kind=kOutput, calls=%fused_computation.4 | convolution fusion | flops 1817333760 | bytes 15888384 | tf_op jit(solution)/shard_map/dot_general | solution.py:272
  254.6 1.6 collective-permute-start.8
  257.5 1.3 collective-permute-start.14
  261.4 1.5 collective-permute-start.17
  262.9 13.5 %collective-permute-done.15 = bf16[128,1344]{0,1:T(8,128)(2,1)S(1)} collective-permute-done((bf16[128,1344]{0,1:T(8,128)(2,1)S(1)}, bf16[128,1344]{0,1:T(8,128)(2,1)S(1)}, u32[]{:S(2)}, u32[]{:S(2)}) %collective-permute-start.15) | collective-permute-done | bytes 344096 | tf_op jit(solution)/shard_map/ppermute | solution.py:25
  276.3 6.3 %collective-permute-done.16 = bf16[128,1344]{0,1:T(8,128)(2,1)S(1)} collective-permute-done((bf16[128,1344]{0,1:T(8,128)(2,1)S(1)}, bf16[128,1344]{0,1:T(8,128)(2,1)S(1)}, u32[]{:S(2)}, u32[]{:S(2)}) %collective-permute-start.16) | collective-permute-done | bytes 344096 | tf_op jit(solution)/shard_map/ppermute | solution.py:25
  282.7 18.2 %collective-permute-done.17 = bf16[128,1344]{0,1:T(8,128)(2,1)S(1)} collective-permute-done((bf16[128,1344]{0,1:T(8,128)(2,1)S(1)}, bf16[128,1344]{0,1:T(8,128)(2,1)S(1)}, u32[]{:S(2)}, u32[]{:S(2)}) %collective-permute-start.17) | collective-permute-done | bytes 344096 | tf_op jit(solution)/shard_map/ppermute | solution.py:25
  301.6 11.4 %convolution_convert_fusion.1 = bf16[128,5280]{0,1:T(8,128)(2,1)S(1)} fusion(bf16[1344,5280]{1,0:T(8,128)(2,1)} %bitcast.81, bf16[128,1344]{0,1:T(8,128)(2,1)S(1)} %bitcast.86, bf16[128,1344]{0,1:T(8,128)(2,1)} %copy-done.19, bf16[128,1344]{0,1:T(8,128)(2,1)} %copy-done.18, bf16[128,1344]{0,1:T(8,128)(2,1)} %copy-done.17, bf16[128,1344]{0,1:T(8,128)(2,1)} %copy-done.16), kind=kOutput, calls=%fused_computation.2 | convolution fusion | flops 1819054080 | bytes 17264640 | tf_op jit(solution)/shard_map/dot_general | solution.py:295
  313.5 2.0 multiply_reduce_fusion.1
  315.6 9.5 %convolution_convert_fusion.5 = bf16[128,1344]{0,1:T(8,128)(2,1)S(1)} fusion(bf16[1344,5280]{1,0:T(8,128)(2,1)} %bitcast.82, f32[128]{0:T(128)S(1)} %add_rsqrt_fusion, bf16[128,5280]{0,1:T(8,128)(2,1)S(1)} %copy-done.4, bf16[128,5280]{0,1:T(8,128)(2,1)} %collective-permute-done.8, bf16[128,5280]{0,1:T(8,128)(2,1)S(1)} %convolution_convert_fusion.3), kind=kOutput, calls=%fused_computation.27 | convolution fusion | flops 1821560832 | bytes 18592256 | tf_op jit(solution)/shard_map/dot_general | solution.py:43
  325.2 3.7 collective-permute-start.9
  328.9 1.3 collective-permute-start.10
  330.2 2.9 collective-permute-start.11
  333.1 2.9 collective-permute-start.12
  336.1 6.8 %collective-permute-done.18 = bf16[128,5280]{0,1:T(8,128)(2,1)S(1)} collective-permute-done((bf16[128,5280]{0,1:T(8,128)(2,1)S(1)}, bf16[128,5280]{0,1:T(8,128)(2,1)S(1)}, u32[]{:S(2)}, u32[]{:S(2)}) %collective-permute-start.18) | collective-permute-done | bytes 1351712 | tf_op jit(solution)/shard_map/ppermute | solution.py:38
  342.8 2.8 multiply_reduce_fusion
  345.7 5.5 %convolution_convert_fusion.4 = bf16[128,1344]{0,1:T(8,128)(2,1)S(1)} fusion(bf16[1344,5280]{1,0:T(8,128)(2,1)S(1)} %bitcast.79, bf16[128,5280]{0,1:T(8,128)(2,1)S(1)} %copy-done.10, bf16[128,5280]{0,1:T(8,128)(2,1)S(1)} %collective-permute-done.18, bf16[128,5280]{0,1:T(8,128)(2,1)S(1)} %convolution_convert_fusion.1, f32[128]{0:T(128)S(1)} %broadcast_multiply_fusion.1, ...), kind=kOutput, calls=%fused_computation.26 | convolution fusion | flops 1826967552 | bytes 22647808 | tf_op jit(solution)/shard_map/dot_general | solution.py:43
  356.5 1.5 collective-permute-start.22
  358.3 1.5 convolution_convert_fusion.10
  359.9 6.5 %collective-permute-done.20 = bf16[128,1344]{0,1:T(8,128)(2,1)S(1)} collective-permute-done((bf16[128,1344]{0,1:T(8,128)(2,1)S(1)}, bf16[128,1344]{0,1:T(8,128)(2,1)S(1)}, u32[]{:S(2)}, u32[]{:S(2)}) %collective-permute-start.20) | collective-permute-done | bytes 344096 | tf_op jit(solution)/shard_map/ppermute | solution.py:25
  366.4 3.8 collective-permute-done.21
  370.2 13.0 %collective-permute-done.22 = bf16[128,1344]{0,1:T(8,128)(2,1)S(1)} collective-permute-done((bf16[128,1344]{0,1:T(8,128)(2,1)S(1)}, bf16[128,1344]{0,1:T(8,128)(2,1)S(1)}, u32[]{:S(2)}, u32[]{:S(2)}) %collective-permute-start.22) | collective-permute-done | bytes 344096 | tf_op jit(solution)/shard_map/ppermute | solution.py:25
  384.0 11.4 %convolution_convert_fusion = bf16[128,5280]{0,1:T(8,128)(2,1)S(1)} fusion(bf16[1344,5280]{1,0:T(8,128)(2,1)} %bitcast.83, bf16[128,1344]{0,1:T(8,128)(2,1)S(1)} %bitcast.85, bf16[128,1344]{0,1:T(8,128)(2,1)} %copy-done.15, bf16[128,1344]{0,1:T(8,128)(2,1)} %copy-done.14, bf16[128,1344]{0,1:T(8,128)(2,1)} %copy-done.13, bf16[128,1344]{0,1:T(8,128)(2,1)} %copy-done.12), kind=kOutput, calls=%fused_computation.1 | convolution fusion | flops 1819054080 | bytes 17264640 | tf_op jit(solution)/shard_map/dot_general | solution.py:295
  396.0 11.1 %convolution_convert_fusion.2 = bf16[128,5280]{0,1:T(8,128)(2,1)} fusion(bf16[128,1344]{0,1:T(8,128)(2,1)S(1)} %bitcast.87, bf16[1344,5280]{1,0:T(8,128)(2,1)} %bitcast.76), kind=kOutput, calls=%fused_computation.3 | convolution fusion | flops 1817333760 | bytes 15888384 | tf_op jit(solution)/shard_map/dot_general | solution.py:272
  407.1 1.5 collective-permute-start.13
  408.6 19.5 %collective-permute-done.23 = bf16[128,5280]{0,1:T(8,128)(2,1)S(1)} collective-permute-done((bf16[128,5280]{0,1:T(8,128)(2,1)S(1)}, bf16[128,5280]{0,1:T(8,128)(2,1)S(1)}, u32[]{:S(2)}, u32[]{:S(2)}) %collective-permute-start.23) | collective-permute-done | bytes 1351712 | tf_op jit(solution)/shard_map/ppermute | solution.py:38
  428.8 25.4 %collective-permute-done.13 = bf16[128,5280]{0,1:T(8,128)(2,1)S(1)} collective-permute-done((bf16[128,5280]{0,1:T(8,128)(2,1)}, bf16[128,5280]{0,1:T(8,128)(2,1)S(1)}, u32[]{:S(2)}, u32[]{:S(2)}) %collective-permute-start.13) | collective-permute-done | bytes 1351712 | tf_op jit(solution)/shard_map/ppermute | solution.py:38
  454.3 4.9 %fusion.8 = (f32[128,5280]{0,1:T(8,128)}, bf16[128,5280]{0,1:T(8,128)(2,1)}) fusion(bf16[128,5280]{0,1:T(8,128)(2,1)S(1)} %copy-done.4, bf16[128,5280]{0,1:T(8,128)(2,1)S(1)} %collective-permute-done.23, bf16[128,5280]{0,1:T(8,128)(2,1)S(1)} %convolution_convert_fusion, f32[128]{0:T(128)S(1)} %broadcast_multiply_fusion, f32[128]{0:T(128)S(1)} %add_rsqrt_fusion.1, ...), kind=kLoop, calls=%fused_computation.18 | loop fusion | flops 18247680 | bytes 17573888 | tf_op jit(solution)/shard_map/add | solution.py:296
  (104 shorter events, 19.4 us)
Async XLA Ops:
  0.6 233.6 %copy-start = (bf16[128,1344]{0,1:T(8,128)(2,1)S(1)}, bf16[128,1344]{0,1:T(8,128)(2,1)}, u32[]{:S(2)}) copy-start(bf16[128,1344]{0,1:T(8,128)(2,1)} %param.8) | copy-start | bytes 1032196
  0.6 181.4 %copy-start.4 = (bf16[128,5280]{0,1:T(8,128)(2,1)S(1)}, bf16[128,5280]{0,1:T(8,128)(2,1)}, u32[]{:S(2)}) copy-start(bf16[128,5280]{0,1:T(8,128)(2,1)} %param.7) | copy-start | bytes 4055044
  2.8 1.2 copy-start.2
  182.0 20.8 %copy-start.20 = (bf16[128,1344]{0,1:T(8,128)(2,1)S(1)}, bf16[128,1344]{0,1:T(8,128)(2,1)}, u32[]{:S(2)}) copy-start(bf16[128,1344]{0,1:T(8,128)(2,1)} %param.9) | copy-start | bytes 1032196
  182.0 24.0 %copy-start.23 = (s32[16]{0:T(128)S(1)}, s32[16]{0:T(128)}, u32[]{:S(2)}) copy-start(s32[16]{0:T(128)} %param.12) | copy-start | bytes 196
  182.1 25.4 %copy-start.9 = (bf16[128,5280]{0,1:T(8,128)(2,1)S(1)}, bf16[128,5280]{0,1:T(8,128)(2,1)}, u32[]{:S(2)}) copy-start(bf16[128,5280]{0,1:T(8,128)(2,1)} %param.13) | copy-start | bytes 4055044
  190.1 25.5 %collective-permute-start = (bf16[128,1344]{0,1:T(8,128)(2,1)}, bf16[128,1344]{0,1:T(8,128)(2,1)}, u32[]{:S(2)}, u32[]{:S(2)}) collective-permute-start(bf16[128,1344]{0,1:T(8,128)(2,1)} %convolution_convert_fusion.6), channel_id=1, source_target_pairs={{0,8},{2,10},{4,12},{6,14},{8,16},{10,18},{12,20},{14,22},{16,24},... | collective-permute-start | bytes 1032200 | tf_op jit(solution)/shard_map/ppermute | solution.py:25
  194.4 26.0 %collective-permute-start.1 = (bf16[128,1344]{0,1:T(8,128)(2,1)}, bf16[128,1344]{0,1:T(8,128)(2,1)}, u32[]{:S(2)}, u32[]{:S(2)}) collective-permute-start(bf16[128,1344]{0,1:T(8,128)(2,1)} %convolution_convert_fusion.6), channel_id=1, source_target_pairs={{0,6},{2,8},{4,10},{6,12},{8,14},{10,16},{12,18},{14,20},{16,22},{... | collective-permute-start | bytes 1032200 | tf_op jit(solution)/shard_map/ppermute | solution.py:25
  196.4 28.1 %collective-permute-start.2 = (bf16[128,1344]{0,1:T(8,128)(2,1)}, bf16[128,1344]{0,1:T(8,128)(2,1)}, u32[]{:S(2)}, u32[]{:S(2)}) collective-permute-start(bf16[128,1344]{0,1:T(8,128)(2,1)} %convolution_convert_fusion.6), channel_id=1, source_target_pairs={{0,4},{2,6},{4,8},{6,10},{8,12},{10,14},{12,16},{14,18},{16,20},{1... | collective-permute-start | bytes 1032200 | tf_op jit(solution)/shard_map/ppermute | solution.py:25
  200.3 27.7 %collective-permute-start.3 = (bf16[128,1344]{0,1:T(8,128)(2,1)}, bf16[128,1344]{0,1:T(8,128)(2,1)}, u32[]{:S(2)}, u32[]{:S(2)}) collective-permute-start(bf16[128,1344]{0,1:T(8,128)(2,1)} %convolution_convert_fusion.6), channel_id=1, source_target_pairs={{0,2},{2,4},{4,6},{6,8},{8,10},{10,12},{12,14},{14,16},{16,18},{18... | collective-permute-start | bytes 1032200 | tf_op jit(solution)/shard_map/ppermute | solution.py:25
  202.8 28.7 %collective-permute-start.4 = (bf16[128,1344]{0,1:T(8,128)(2,1)S(1)}, bf16[128,1344]{0,1:T(8,128)(2,1)}, u32[]{:S(2)}, u32[]{:S(2)}) collective-permute-start(bf16[128,1344]{0,1:T(8,128)(2,1)S(1)} %copy-done.20), channel_id=1, source_target_pairs={{0,8},{2,10},{4,12},{6,14},{8,16},{10,18},{12,20},{14,22},{16,24},... | collective-permute-start | bytes 1032200 | tf_op jit(solution)/shard_map/ppermute | solution.py:25
  215.7 17.0 %collective-permute-start.5 = (bf16[128,1344]{0,1:T(8,128)(2,1)S(1)}, bf16[128,1344]{0,1:T(8,128)(2,1)S(1)}, u32[]{:S(2)}, u32[]{:S(2)}) collective-permute-start(bf16[128,1344]{0,1:T(8,128)(2,1)S(1)} %copy-done.20), channel_id=1, source_target_pairs={{0,6},{2,8},{4,10},{6,12},{8,14},{10,16},{12,18},{14,20},{16,22},{... | collective-permute-start | bytes 1032200 | tf_op jit(solution)/shard_map/ppermute | solution.py:25
  220.4 12.3 %collective-permute-start.6 = (bf16[128,1344]{0,1:T(8,128)(2,1)S(1)}, bf16[128,1344]{0,1:T(8,128)(2,1)S(1)}, u32[]{:S(2)}, u32[]{:S(2)}) collective-permute-start(bf16[128,1344]{0,1:T(8,128)(2,1)S(1)} %copy-done.20), channel_id=1, source_target_pairs={{0,4},{2,6},{4,8},{6,10},{8,12},{10,14},{12,16},{14,18},{16,20},{1... | collective-permute-start | bytes 1032200 | tf_op jit(solution)/shard_map/ppermute | solution.py:25
  224.6 8.3 %collective-permute-start.7 = (bf16[128,1344]{0,1:T(8,128)(2,1)S(1)}, bf16[128,1344]{0,1:T(8,128)(2,1)S(1)}, u32[]{:S(2)}, u32[]{:S(2)}) collective-permute-start(bf16[128,1344]{0,1:T(8,128)(2,1)S(1)} %copy-done.20), channel_id=1, source_target_pairs={{0,2},{2,4},{4,6},{6,8},{8,10},{10,12},{12,14},{14,16},{16,18},{18... | collective-permute-start | bytes 1032200 | tf_op jit(solution)/shard_map/ppermute | solution.py:25
  244.8 11.4 %copy-start.21 = (bf16[1344,128]{1,0:T(8,128)(2,1)S(1)}, bf16[1344,128]{1,0:T(8,128)(2,1)}, u32[]{:S(2)}) copy-start(bf16[1344,128]{1,0:T(8,128)(2,1)} %convolution_convert_fusion.7) | copy-start | bytes 1032196
  254.6 58.9 %collective-permute-start.8 = (bf16[128,5280]{0,1:T(8,128)(2,1)S(1)}, bf16[128,5280]{0,1:T(8,128)(2,1)}, u32[]{:S(2)}, u32[]{:S(2)}) collective-permute-start(bf16[128,5280]{0,1:T(8,128)(2,1)S(1)} %convolution_convert_fusion.3), channel_id=1, source_target_pairs={{0,1},{1,0},{2,3},{3,2},{4,5},{5,4},{6,7},{7,6},{8,9},{9,8},{10,11... | collective-permute-start | bytes 4055048 | tf_op jit(solution)/shard_map/ppermute | solution.py:38
  257.5 5.4 %collective-permute-start.14 = (bf16[128,1344]{0,1:T(8,128)(2,1)S(1)}, bf16[128,1344]{0,1:T(8,128)(2,1)S(1)}, u32[]{:S(2)}, u32[]{:S(2)}) collective-permute-start(bf16[128,1344]{0,1:T(8,128)(2,1)S(1)} %bitcast.97), channel_id=1, source_target_pairs={{2,0},{4,2},{6,4},{8,6},{10,8},{12,10},{14,12},{16,14},{18,16},{20... | collective-permute-start | bytes 1032200 | tf_op jit(solution)/shard_map/ppermute | solution.py:25
  258.8 17.6 %collective-permute-start.15 = (bf16[128,1344]{0,1:T(8,128)(2,1)S(1)}, bf16[128,1344]{0,1:T(8,128)(2,1)S(1)}, u32[]{:S(2)}, u32[]{:S(2)}) collective-permute-start(bf16[128,1344]{0,1:T(8,128)(2,1)S(1)} %bitcast.96), channel_id=1, source_target_pairs={{4,0},{6,2},{8,4},{10,6},{12,8},{14,10},{16,12},{18,14},{20,16},{2... | collective-permute-start | bytes 1032200 | tf_op jit(solution)/shard_map/ppermute | solution.py:25
  260.1 22.6 %collective-permute-start.16 = (bf16[128,1344]{0,1:T(8,128)(2,1)S(1)}, bf16[128,1344]{0,1:T(8,128)(2,1)S(1)}, u32[]{:S(2)}, u32[]{:S(2)}) collective-permute-start(bf16[128,1344]{0,1:T(8,128)(2,1)S(1)} %bitcast.95), channel_id=1, source_target_pairs={{6,0},{8,2},{10,4},{12,6},{14,8},{16,10},{18,12},{20,14},{22,16},{... | collective-permute-start | bytes 1032200 | tf_op jit(solution)/shard_map/ppermute | solution.py:25
  261.4 39.5 %collective-permute-start.17 = (bf16[128,1344]{0,1:T(8,128)(2,1)S(1)}, bf16[128,1344]{0,1:T(8,128)(2,1)S(1)}, u32[]{:S(2)}, u32[]{:S(2)}) collective-permute-start(bf16[128,1344]{0,1:T(8,128)(2,1)S(1)} %bitcast.94), channel_id=1, source_target_pairs={{8,0},{10,2},{12,4},{14,6},{16,8},{18,10},{20,12},{22,14},{24,16},... | collective-permute-start | bytes 1032200 | tf_op jit(solution)/shard_map/ppermute | solution.py:25
  262.9 38.0 %copy-start.16 = (bf16[128,1344]{0,1:T(8,128)(2,1)}, bf16[128,1344]{0,1:T(8,128)(2,1)S(1)}, u32[]{:S(2)}) copy-start(bf16[128,1344]{0,1:T(8,128)(2,1)S(1)} %collective-permute-done.14) | copy-start | bytes 1032196
  276.3 24.5 %copy-start.17 = (bf16[128,1344]{0,1:T(8,128)(2,1)}, bf16[128,1344]{0,1:T(8,128)(2,1)S(1)}, u32[]{:S(2)}) copy-start(bf16[128,1344]{0,1:T(8,128)(2,1)S(1)} %collective-permute-done.15) | copy-start | bytes 1032196
  282.7 18.2 %copy-start.18 = (bf16[128,1344]{0,1:T(8,128)(2,1)}, bf16[128,1344]{0,1:T(8,128)(2,1)S(1)}, u32[]{:S(2)}) copy-start(bf16[128,1344]{0,1:T(8,128)(2,1)S(1)} %collective-permute-done.16) | copy-start | bytes 1032196
  313.0 29.9 %collective-permute-start.18 = (bf16[128,5280]{0,1:T(8,128)(2,1)S(1)}, bf16[128,5280]{0,1:T(8,128)(2,1)S(1)}, u32[]{:S(2)}, u32[]{:S(2)}) collective-permute-start(bf16[128,5280]{0,1:T(8,128)(2,1)S(1)} %convolution_convert_fusion.1), channel_id=1, source_target_pairs={{0,1},{1,0},{2,3},{3,2},{4,5},{5,4},{6,7},{7,6},{8,9},{9,8},{10,11... | collective-permute-start | bytes 4055048 | tf_op jit(solution)/shard_map/ppermute | solution.py:38
  315.6 30.1 %slice-start = ((s8[14450688]{0:T(1024)(128)(4,1)}), s8[4194304]{0:T(1024)(128)(4,1)S(1)}, s32[]{:S(2)}) async-start(s8[14450688]{0:T(1024)(128)(4,1)} %bitcast.77), calls=%async_computation | async-start | bytes 8388608
  315.6 30.0 %slice-start.1 = ((s8[14450688]{0:T(1024)(128)(4,1)}), s8[4194304]{0:T(1024)(128)(4,1)S(1)}, s32[]{:S(2)}) async-start(s8[14450688]{0:T(1024)(128)(4,1)} %bitcast.77), calls=%async_computation.1 | async-start | bytes 8388608
  315.6 30.0 %slice-start.2 = ((s8[14450688]{0:T(1024)(128)(4,1)}), s8[4194304]{0:T(1024)(128)(4,1)S(1)}, s32[]{:S(2)}) async-start(s8[14450688]{0:T(1024)(128)(4,1)} %bitcast.77), calls=%async_computation.2 | async-start | bytes 8388608
  315.6 30.0 %slice-start.3 = ((s8[14450688]{0:T(1024)(128)(4,1)}), s8[1867776]{0:T(1024)(128)(4,1)S(1)}, s32[]{:S(2)}) async-start(s8[14450688]{0:T(1024)(128)(4,1)} %bitcast.77), calls=%async_computation.3 | async-start | bytes 3735552
  325.2 20.5 %copy-start.10 = (bf16[128,5280]{0,1:T(8,128)(2,1)S(1)}, bf16[128,5280]{0,1:T(8,128)(2,1)}, u32[]{:S(2)}) copy-start(bf16[128,5280]{0,1:T(8,128)(2,1)} %param.13) | copy-start | bytes 4055044
  325.2 28.5 %collective-permute-start.9 = (bf16[128,1344]{0,1:T(8,128)(2,1)S(1)}, bf16[128,1344]{0,1:T(8,128)(2,1)S(1)}, u32[]{:S(2)}, u32[]{:S(2)}) collective-permute-start(bf16[128,1344]{0,1:T(8,128)(2,1)S(1)} %convolution_convert_fusion.5), channel_id=1, source_target_pairs={{0,8},{2,10},{4,12},{6,14},{8,16},{10,18},{12,20},{14,22},{16,24},... | collective-permute-start | bytes 1032200 | tf_op jit(solution)/shard_map/ppermute | solution.py:25
  328.9 26.2 %collective-permute-start.10 = (bf16[128,1344]{0,1:T(8,128)(2,1)S(1)}, bf16[128,1344]{0,1:T(8,128)(2,1)S(1)}, u32[]{:S(2)}, u32[]{:S(2)}) collective-permute-start(bf16[128,1344]{0,1:T(8,128)(2,1)S(1)} %convolution_convert_fusion.5), channel_id=1, source_target_pairs={{0,6},{2,8},{4,10},{6,12},{8,14},{10,16},{12,18},{14,20},{16,22},{... | collective-permute-start | bytes 1032200 | tf_op jit(solution)/shard_map/ppermute | solution.py:25
  330.2 26.3 %collective-permute-start.11 = (bf16[128,1344]{0,1:T(8,128)(2,1)S(1)}, bf16[128,1344]{0,1:T(8,128)(2,1)S(1)}, u32[]{:S(2)}, u32[]{:S(2)}) collective-permute-start(bf16[128,1344]{0,1:T(8,128)(2,1)S(1)} %convolution_convert_fusion.5), channel_id=1, source_target_pairs={{0,4},{2,6},{4,8},{6,10},{8,12},{10,14},{12,16},{14,18},{16,20},{1... | collective-permute-start | bytes 1032200 | tf_op jit(solution)/shard_map/ppermute | solution.py:25
  333.1 25.0 %collective-permute-start.12 = (bf16[128,1344]{0,1:T(8,128)(2,1)S(1)}, bf16[128,1344]{0,1:T(8,128)(2,1)S(1)}, u32[]{:S(2)}, u32[]{:S(2)}) collective-permute-start(bf16[128,1344]{0,1:T(8,128)(2,1)S(1)} %convolution_convert_fusion.5), channel_id=1, source_target_pairs={{0,2},{2,4},{4,6},{6,8},{8,10},{10,12},{12,14},{14,16},{16,18},{18... | collective-permute-start | bytes 1032200 | tf_op jit(solution)/shard_map/ppermute | solution.py:25
  342.8 2.8 copy-start.5
  352.4 7.4 %collective-permute-start.19 = (bf16[128,1344]{0,1:T(8,128)(2,1)S(1)}, bf16[128,1344]{0,1:T(8,128)(2,1)S(1)}, u32[]{:S(2)}, u32[]{:S(2)}) collective-permute-start(bf16[128,1344]{0,1:T(8,128)(2,1)S(1)} %bitcast.93), channel_id=1, source_target_pairs={{2,0},{4,2},{6,4},{8,6},{10,8},{12,10},{14,12},{16,14},{18,16},{20... | collective-permute-start | bytes 1032200 | tf_op jit(solution)/shard_map/ppermute | solution.py:25
  353.7 12.7 %collective-permute-start.20 = (bf16[128,1344]{0,1:T(8,128)(2,1)S(1)}, bf16[128,1344]{0,1:T(8,128)(2,1)S(1)}, u32[]{:S(2)}, u32[]{:S(2)}) collective-permute-start(bf16[128,1344]{0,1:T(8,128)(2,1)S(1)} %bitcast.92), channel_id=1, source_target_pairs={{4,0},{6,2},{8,4},{10,6},{12,8},{14,10},{16,12},{18,14},{20,16},{2... | collective-permute-start | bytes 1032200 | tf_op jit(solution)/shard_map/ppermute | solution.py:25
  355.1 15.1 %collective-permute-start.21 = (bf16[128,1344]{0,1:T(8,128)(2,1)S(1)}, bf16[128,1344]{0,1:T(8,128)(2,1)S(1)}, u32[]{:S(2)}, u32[]{:S(2)}) collective-permute-start(bf16[128,1344]{0,1:T(8,128)(2,1)S(1)} %bitcast.91), channel_id=1, source_target_pairs={{6,0},{8,2},{10,4},{12,6},{14,8},{16,10},{18,12},{20,14},{22,16},{... | collective-permute-start | bytes 1032200 | tf_op jit(solution)/shard_map/ppermute | solution.py:25
  356.5 26.8 %collective-permute-start.22 = (bf16[128,1344]{0,1:T(8,128)(2,1)S(1)}, bf16[128,1344]{0,1:T(8,128)(2,1)S(1)}, u32[]{:S(2)}, u32[]{:S(2)}) collective-permute-start(bf16[128,1344]{0,1:T(8,128)(2,1)S(1)} %bitcast.90), channel_id=1, source_target_pairs={{8,0},{10,2},{12,4},{14,6},{16,8},{18,10},{20,12},{22,14},{24,16},... | collective-permute-start | bytes 1032200 | tf_op jit(solution)/shard_map/ppermute | solution.py:25
  359.9 23.4 %copy-start.12 = (bf16[128,1344]{0,1:T(8,128)(2,1)}, bf16[128,1344]{0,1:T(8,128)(2,1)S(1)}, u32[]{:S(2)}) copy-start(bf16[128,1344]{0,1:T(8,128)(2,1)S(1)} %collective-permute-done.19) | copy-start | bytes 1032196
  366.4 16.9 %copy-start.13 = (bf16[128,1344]{0,1:T(8,128)(2,1)}, bf16[128,1344]{0,1:T(8,128)(2,1)S(1)}, u32[]{:S(2)}) copy-start(bf16[128,1344]{0,1:T(8,128)(2,1)S(1)} %collective-permute-done.20) | copy-start | bytes 1032196
  370.2 13.1 %copy-start.14 = (bf16[128,1344]{0,1:T(8,128)(2,1)}, bf16[128,1344]{0,1:T(8,128)(2,1)S(1)}, u32[]{:S(2)}) copy-start(bf16[128,1344]{0,1:T(8,128)(2,1)S(1)} %collective-permute-done.21) | copy-start | bytes 1032196
  384.0 12.0 %copy-start.8 = (bf16[14,96,128]{2,1,0:T(8,128)(2,1)S(1)}, bf16[14,96,128]{2,1,0:T(8,128)(2,1)}, u32[]{:S(2)}) copy-start(bf16[14,96,128]{2,1,0:T(8,128)(2,1)} %convolution_convert_fusion.10) | copy-start | bytes 1032196
  395.4 32.7 %collective-permute-start.23 = (bf16[128,5280]{0,1:T(8,128)(2,1)S(1)}, bf16[128,5280]{0,1:T(8,128)(2,1)S(1)}, u32[]{:S(2)}, u32[]{:S(2)}) collective-permute-start(bf16[128,5280]{0,1:T(8,128)(2,1)S(1)} %convolution_convert_fusion), channel_id=1, source_target_pairs={{0,1},{1,0},{2,3},{3,2},{4,5},{5,4},{6,7},{7,6},{8,9},{9,8},{10,11... | collective-permute-start | bytes 4055048 | tf_op jit(solution)/shard_map/ppermute | solution.py:38
  407.0 47.2 %copy-start.6 = (bf16[128,5280]{0,1:T(8,128)(2,1)S(1)}, bf16[128,5280]{0,1:T(8,128)(2,1)}, u32[]{:S(2)}) copy-start(bf16[128,5280]{0,1:T(8,128)(2,1)} %copy-done.5) | copy-start | bytes 4055044
  407.0 47.2 %copy-start.7 = (bf16[128,5280]{0,1:T(8,128)(2,1)S(1)}, bf16[128,5280]{0,1:T(8,128)(2,1)}, u32[]{:S(2)}) copy-start(bf16[128,5280]{0,1:T(8,128)(2,1)} %convolution_convert_fusion.2) | copy-start | bytes 4055044
  407.1 47.2 %copy-start.11 = (bf16[128,5280]{0,1:T(8,128)(2,1)S(1)}, bf16[128,5280]{0,1:T(8,128)(2,1)}, u32[]{:S(2)}) copy-start(bf16[128,5280]{0,1:T(8,128)(2,1)} %param.13) | copy-start | bytes 4055044
  407.1 47.2 %collective-permute-start.13 = (bf16[128,5280]{0,1:T(8,128)(2,1)}, bf16[128,5280]{0,1:T(8,128)(2,1)S(1)}, u32[]{:S(2)}, u32[]{:S(2)}) collective-permute-start(bf16[128,5280]{0,1:T(8,128)(2,1)} %convolution_convert_fusion.2), channel_id=1, source_target_pairs={{0,1},{1,0},{2,3},{3,2},{4,5},{5,4},{6,7},{7,6},{8,9},{9,8},{10,11... | collective-permute-start | bytes 4055048 | tf_op jit(solution)/shard_map/ppermute | solution.py:38
  454.3 4.9 %copy-start.1 = (bf16[128,1344]{0,1:T(8,128)(2,1)S(1)}, bf16[128,1344]{0,1:T(8,128)(2,1)}, u32[]{:S(2)}) copy-start(bf16[128,1344]{0,1:T(8,128)(2,1)} %param.8) | copy-start | bytes 1032196
  (4 other events, 3.8 us)
